TPU v7x, 32 devices: a whole 2x2x4 slice. The times are simulated.
32 devices in a mesh: scene: 2 (over y), bins: 4 (over z), az: 4 (over x, core).
Axes of the slice: x: 2, y: 2, z: 4, core: 2. Of those that a mesh axis runs over, the one named last changes fastest.
Arguments:
- raw_echoes: bfloat16 [2, 8, 512, 16384], P(None, ('scene', 'az'), 'bins'), parts along dimension 1, may hold values from -6 to 6
- range_phase: float32 [16384], replicated, may hold values from -3.140625 to 3.140625
- band_start: int32 [16384], replicated, may hold values from 0 to 16447, as said below
- band_weight: bfloat16 [8, 16384], replicated, may hold values from -0.25 to 0.75
- intersection_length: int32 [16384], P('bins'), may hold values from 32 to 128
- azimuth_rate: float32 [16384], P('bins'), may hold values from 0.25 to 2
Outputs:
- focused_image: bfloat16 [2, 8, 512, 16384], P(None, ('scene', 'az'), None, 'bins'), parts along dimension 1
There are 2 independent parts, one for each index of `scene`. A program takes and returns all parts, laid end to end along the dimension named above; an argument that names none is the same for every part. Nothing has to cross between parts.
Inputs may be any that keep to these rules, and one draw needn't show every extreme that they name: band_start[b] - b lies between 0 and 64 for every range bin b.
All inputs are finite; a program needn't handle non-finite values.
Results may differ from a plain program's by a relative error of at most 0.02.
Values may be sent and summed in bfloat16 or wider, within the bound.
No kernel may reach another device: no remote copies, remote signals or barrier semaphores. Data moves between devices by JAX's collectives and lax.ppermute only.
A program may use at most 128 MiB of HBM per device.

v0:
```python
import math

import jax
import jax.numpy as jnp
from jax import lax
from jax.sharding import PartitionSpec as P

OVLMAX = 128


def passed_along(value, axis, steps):
    count = lax.axis_size(axis)
    first, last = (max(0, -steps), min(count, count - steps))
    return lax.ppermute(value, axis, [(source, source + steps) for source in range(first, last)])


def phase_pair(row_count, col_count, length, direction):
    row_index = jnp.arange(row_count, dtype=jnp.int32)[:, None]
    col_index = jnp.arange(col_count, dtype=jnp.int32)[None, :]
    product = (row_index * col_index % length).astype(jnp.float32)
    phase_angle = product * (direction * 2.0 * math.pi / length)
    return (jnp.cos(phase_angle), jnp.sin(phase_angle))


def narrow_pair(operands):
    return (operands[0].astype(jnp.bfloat16), operands[1].astype(jnp.bfloat16))


def complex_product(form, left_pair, right_pair):
    left_real, left_imag = left_pair
    right_real, right_imag = right_pair
    real_part = jnp.einsum(
        form, left_real, right_real, preferred_element_type=jnp.float32
    ) - jnp.einsum(form, left_imag, right_imag, preferred_element_type=jnp.float32)
    imag_part = jnp.einsum(
        form, left_real, right_imag, preferred_element_type=jnp.float32
    ) + jnp.einsum(form, left_imag, right_real, preferred_element_type=jnp.float32)
    return (real_part, imag_part)


def complex_scale(operands, cosine, sine_part):
    real_part = operands[0] * cosine - operands[1] * sine_part
    imag_part = operands[0] * sine_part + operands[1] * cosine
    return (real_part, imag_part)


def compress_lines(echo_lines, range_phase):
    line_count, line_width = (echo_lines.shape[1], echo_lines.shape[2])
    radix_size = 128
    other_size = line_width // radix_size
    line_grid = echo_lines.reshape(2, line_count, radix_size, other_size)
    first_table = narrow_pair(phase_pair(radix_size, radix_size, radix_size, -1.0))
    partial_value = complex_product("ka,pan->pkn", first_table, (line_grid[0], line_grid[1]))
    partial_value = complex_scale(
        partial_value, *phase_pair(radix_size, other_size, line_width, -1.0)
    )
    second_table = narrow_pair(phase_pair(other_size, other_size, other_size, -1.0))
    spectrum = complex_product("pkn,nm->pkm", narrow_pair(partial_value), second_table)
    filter_angle = range_phase.reshape(other_size, radix_size).T
    filtered = narrow_pair(complex_scale(spectrum, jnp.cos(filter_angle), -jnp.sin(filter_angle)))
    back_table = narrow_pair(phase_pair(other_size, other_size, other_size, 1.0))
    partial_value = complex_product("pkm,mn->pkn", filtered, back_table)
    partial_value = complex_scale(
        partial_value, *phase_pair(radix_size, other_size, line_width, 1.0)
    )
    last_table = narrow_pair(phase_pair(radix_size, radix_size, radix_size, 1.0))
    result = complex_product("ak,pkn->pan", last_table, narrow_pair(partial_value))
    stacked = jnp.stack(result) * (1.0 / line_width)
    return stacked.reshape(2, line_count, line_width).astype(jnp.bfloat16)


def migrate(samples, range_rim, starts, weights):
    row_count, line_width = (samples.shape[1], samples.shape[2])
    blocks = line_width // 128
    extended = jnp.concatenate([samples, range_rim], axis=2)
    windows = jnp.concatenate(
        [
            extended[:, :, :line_width].reshape(2, row_count, blocks, 128),
            extended[:, :, 128:].reshape(2, row_count, blocks, 128),
        ],
        axis=3,
    )
    block_start = 128 * jnp.arange(blocks, dtype=jnp.int32)[:, None]
    offsets = starts.reshape(blocks, 128) - block_start
    position = jnp.arange(256, dtype=jnp.int32)[None, :, None]
    band_matrix = jnp.zeros((blocks, 256, 128), jnp.bfloat16)
    for tap_index in range(weights.shape[0]):
        tap_weight = weights[tap_index].reshape(blocks, 128)[:, None, :]
        band_matrix = band_matrix + jnp.where(
            position == (offsets + tap_index)[:, None, :], tap_weight, jnp.zeros((), jnp.bfloat16)
        )
    result = jnp.einsum("sprj,rjk->sprk", windows, band_matrix, preferred_element_type=jnp.float32)
    return result.reshape(2, row_count, line_width).astype(jnp.bfloat16)


def shards(raw_echoes, range_phase, band_start, band_weight, intersection_length, azimuth_rate):
    echo_lines = raw_echoes[:, 0]
    compressed = compress_lines(echo_lines, range_phase)
    empty_rim = jnp.zeros((2, compressed.shape[1], 128), jnp.bfloat16)
    outgoing = migrate(compressed, empty_rim, band_start, band_weight)
    turned = lax.all_to_all(outgoing, "bins", split_axis=2, concat_axis=1, tiled=True)
    head_lines = passed_along(turned[:, :OVLMAX], "az", -1)
    aperture = jnp.concatenate([turned, head_lines], axis=1)
    own_count = turned.shape[1]
    length = aperture.shape[1]
    pulses = jnp.arange(length, dtype=jnp.int32)[:, None]
    inside = (pulses < own_count) | (pulses - own_count < intersection_length[None, :])
    aperture = jnp.where(inside[None], aperture, jnp.zeros((), jnp.bfloat16))
    forward_table = narrow_pair(phase_pair(length, length, length, -1.0))
    spectrum = complex_product("fp,pr->fr", forward_table, (aperture[0], aperture[1]))
    doppler = jnp.arange(length, dtype=jnp.int32)
    signed = jnp.where(2 * doppler >= length, doppler - length, doppler).astype(jnp.float32)
    phase_angle = math.pi * azimuth_rate[None, :] * (signed * signed)[:, None] / length
    focused = narrow_pair(complex_scale(spectrum, jnp.cos(phase_angle), -jnp.sin(phase_angle)))
    inverse_table = narrow_pair(phase_pair(own_count, length, length, 1.0))
    image_pair = complex_product("qf,fr->qr", inverse_table, focused)
    stacked = jnp.stack(image_pair) * (1.0 / length)
    return stacked.astype(jnp.bfloat16)[:, None]


def solution(mesh):
    in_specs = (P(None, ("scene", "az"), "bins", None), P(), P(), P(), P("bins"), P("bins"))
    out_specs = P(None, ("scene", "az"), None, "bins")
    return jax.shard_map(shards, mesh=mesh, in_specs=in_specs, out_specs=out_specs, check_vma=False)
```

profile of v0, /device:TPU:1, one launch (start us, length us, event | category | flops | bytes accessed | tf_op | source)
XLA Modules:
  0.0 641.5 jit_solution(2054546862084710419)
XLA Ops:
  0.0 3.9 slice_bitcast_fusion.7
  3.9 1.2 copy.55
  5.1 4.9 fusion.105
  10.0 4.7 fusion.99
  14.7 0.3 multiply_sine_fusion.1
  15.0 1.2 copy.54
  16.2 4.7 fusion.97
  20.9 10.6 %fusion.42 = (bf16[128,128,128]{2,1,0:T(8,128)(2,1)S(1)}, bf16[128,128,128]{2,1,0:T(8,128)(2,1)S(1)}) fusion(f32[128,128]{1,0:T(8,128)S(1)} %get-tuple-element.37, f32[128,128]{1,0:T(8,128)S(1)} %get-tuple-element.38, f32[128,128,128]{2,0,1:T(8,128)} %fusion.105, f32[128,128,128]{2,0,1:T(8,128)} %fusion.97, f32[128,128,128]{2,0,1:T(8,128)} %fusion.99, ...), kind=kOutput, calls=%fused_computation.64 | convolution fusion | flops 558088192 | bytes 37879808 | tf_op jit(solution)/shard_map/ka,pan->pkn/dot_general | solution.py:32
  31.5 4.9 fusion.101
  36.4 4.7 fusion.95
  41.1 4.7 fusion.103
  45.8 0.2 cosine_bitcast_fusion
  46.0 0.1 copy.35
  46.1 0.1 copy.36
  46.2 13.0 %add_convert_fusion.2 = (bf16[128,128,128]{2,1,0:T(8,128)(2,1)S(1)}, bf16[128,128,128]{2,1,0:T(8,128)(2,1)S(1)}) fusion(f32[128,128]{1,0:T(8,128)S(1)} %copy.36, f32[128,128]{1,0:T(8,128)S(1)} %copy.35, f32[128,128,128]{2,1,0:T(8,128)} %fusion.101, f32[128,128,128]{2,1,0:T(8,128)} %fusion.103, f32[128,128,128]{2,1,0:T(8,128)} %fusion.95, ...), kind=kOutput, calls=%fused_computation.45 | convolution fusion | flops 558088192 | bytes 37879808 | tf_op jit(solution)/shard_map/pkn,nm->pkm/dot_general | solution.py:35
  59.2 4.7 fusion.83
  63.9 4.9 fusion.89
  68.8 0.3 multiply_sine_fusion
  69.1 4.7 fusion.91
  73.8 12.9 %subtract_convert_fusion.1 = (bf16[128,128,128]{2,1,0:T(8,128)(2,1)}, bf16[128,128,128]{2,1,0:T(8,128)(2,1)S(1)}) fusion(f32[128,128]{1,0:T(8,128)S(1)} %get-tuple-element.39, f32[128,128]{1,0:T(8,128)S(1)} %get-tuple-element.40, f32[128,128,128]{2,1,0:T(8,128)} %fusion.89, f32[128,128,128]{2,1,0:T(8,128)} %fusion.91, f32[128,128,128]{2,1,0:T(8,128)} %fusion.83, ...), kind=kOutput, calls=%fused_computation.44 | convolution fusion | flops 558088192 | bytes 37879808 | tf_op jit(solution)/shard_map/pkm,mn->pkn/dot_general | solution.py:35
  86.7 4.9 fusion.79
  91.6 1.5 fusion.77
  93.1 10.6 %subtract_bitcast_fusion.1 = (f32[1,128,128,128]{2,3,1,0:T(8,128)}, f32[128,128,128]{1,2,0:T(8,128)}) fusion(f32[128,128,128]{2,1,0:T(8,128)} %fusion.79, bf16[128,128,128]{2,1,0:T(8,128)(2,1)S(1)} %copy-done.1), kind=kOutput, calls=%fused_computation.78 | convolution fusion | flops 539213824 | bytes 29360128 | tf_op jit(solution)/shard_map/ak,pkn->pan/dot_general | solution.py:32
  103.7 7.5 %add_bitcast_fusion.1 = (f32[1,128,128,128]{2,3,1,0:T(8,128)}, f32[128,128,128]{1,2,0:T(8,128)}) fusion(f32[128,128,128]{2,1,0:T(8,128)S(1)} %fusion.77, bf16[128,128,128]{2,1,0:T(8,128)(2,1)S(1)} %get-tuple-element.16), kind=kOutput, calls=%fused_computation.76 | convolution fusion | flops 539213824 | bytes 29360128 | tf_op jit(solution)/shard_map/ak,pkn->pan/dot_general | solution.py:35
  111.2 9.4 %copy.41 = f32[128,128,128]{0,2,1:T(8,128)} copy(f32[128,128,128]{1,2,0:T(8,128)} %get-tuple-element.24) | data formatting | bytes 16777216 | tf_op jit(solution)/shard_map/sub | solution.py:32
  120.6 9.4 %copy.42 = f32[128,128,128]{0,2,1:T(8,128)} copy(f32[128,128,128]{1,2,0:T(8,128)} %get-tuple-element.26) | data formatting | bytes 16777216 | tf_op jit(solution)/shard_map/add | solution.py:35
  130.1 6.7 %fusion.1 = bf16[2,128,16384]{1,2,0:T(8,128)(2,1)S(1)} fusion(f32[1,128,16384]{1,2,0:T(8,128)} %bitcast.146, f32[1,128,16384]{1,2,0:T(8,128)} %bitcast.145), kind=kLoop, calls=%fused_computation.3 | loop fusion | flops 12582912 | bytes 25165824 | tf_op jit(solution)/shard_map/convert_element_type | solution.py:69
  136.7 3.7 pad_slice_fusion
  140.4 13.6 %copy.43 = bf16[2,128,128,128]{2,3,1,0:T(8,128)(2,1)} copy(bf16[2,128,128,128]{1,3,2,0:T(8,128)(2,1)} %bitcast.147) | data formatting | bytes 16777216 | tf_op jit(solution)/shard_map/reshape | solution.py:79
  154.0 7.1 %fusion = bf16[2,128,128,128]{2,3,1,0:T(8,128)(2,1)S(1)} fusion(f32[1,128,128,128]{2,3,1,0:T(8,128)} %get-tuple-element.25, f32[1,128,128,128]{2,3,1,0:T(8,128)} %get-tuple-element.23), kind=kLoop, calls=%fused_computation.1 | loop fusion | flops 12582912 | bytes 25165824 | tf_op jit(solution)/shard_map/convert_element_type | solution.py:69
  161.1 1.1 copy-done.2
  162.2 6.5 %pad_maximum_fusion = bf16[2,128,128,256]{2,3,1,0:T(8,128)(2,1)} fusion(bf16[2,128,128,128]{2,3,1,0:T(8,128)(2,1)S(1)} %copy-done.2, bf16[2,128,128,128]{2,3,1,0:T(8,128)(2,1)S(1)} %fusion), kind=kLoop, calls=%fused_computation.4 | loop fusion | flops 33554432 | bytes 33554432 | tf_op jit(solution)/shard_map/concatenate | solution.py:76
  168.7 23.6 %copy.44 = bf16[2,128,128,256]{3,1,0,2:T(8,128)(2,1)} copy(bf16[2,128,128,256]{2,3,1,0:T(8,128)(2,1)} %pad_maximum_fusion) | data formatting | bytes 33554432 | tf_op jit(solution)/shard_map/concatenate | solution.py:76
  192.4 0.1 broadcast_add_fusion.6
  192.5 1.4 slice_reduce_fusion.7
  193.9 38.2 %fusion.232 = bf16[128,256,128,1]{1,2,3,0:T(8,128)(2,1)} fusion(s32[128,128]{1,0:T(8,128)S(1)} %get-tuple-element.34, s32[128,128]{1,0:T(8,128)S(1)} %get-tuple-element.30, s32[128,128]{1,0:T(8,128)S(1)} %get-tuple-element.31, s32[128,128]{1,0:T(8,128)S(1)} %get-tuple-element.32, s32[128,128]{1,0:T(8,128)S(1)} %get-tuple-element.33, ...), kind=kLoop, calls=%fused_computation.32.clone.clone.clone.clone.1 | loop fusion | flops 134217728 | bytes 9175040 | tf_op jit(solution)/shard_map/sprj,rjk->sprk/dot_general | solution.py:92
  232.1 13.1 %convert_bitcast_fusion = bf16[2,128,128,128]{1,3,0,2:T(8,128)(2,1)} fusion(bf16[2,128,128,256]{3,1,0,2:T(8,128)(2,1)} %copy.44, bf16[128,256,128,1]{1,2,3,0:T(8,128)(2,1)} %fusion.232), kind=kOutput, calls=%fused_computation.42 | convolution fusion | flops 2151677952 | bytes 33554432 | tf_op jit(solution)/shard_map/sprj,rjk->sprk/dot_general | solution.py:92
  245.2 10.5 %copy.45 = bf16[2,128,128,128]{1,3,2,0:T(8,128)(2,1)} copy(bf16[2,128,128,128]{1,3,0,2:T(8,128)(2,1)} %convert_bitcast_fusion) | data formatting | bytes 16777216 | tf_op jit(solution)/shard_map/convert_element_type | solution.py:93
  255.7 15.6 %copy.46 = bf16[2,128,16384]{1,0,2:T(2,128)(2,1)S(1)} copy(bf16[2,128,16384]{1,2,0:T(8,128)(2,1)} %bitcast.148) | data formatting | bytes 16777216 | tf_op jit(solution)/shard_map/convert_element_type | solution.py:93
  271.3 187.4 %all_to_all.18 = bf16[2,128,16384]{1,0,2:T(2,128)(2,1)S(1)} all-to-all(bf16[2,128,16384]{1,0,2:T(2,128)(2,1)S(1)} %copy.46), channel_id=1, replica_groups=mesh['scene'=2,'bins'=4,'az'=4] {'bins'}, dimensions={2} | all-to-all | bytes 16777216 | tf_op jit(solution)/shard_map/all_to_all | solution.py:101
  458.7 10.5 %copy.47 = bf16[2,128,16384]{1,2,0:T(8,128)(2,1)} copy(bf16[2,128,16384]{1,0,2:T(2,128)(2,1)S(1)} %all_to_all.18) | data formatting | bytes 16777216 | tf_op jit(solution)/shard_map/all_to_all | solution.py:101
  469.2 12.1 %copy.48 = bf16[2,4,128,4096]{3,2,1,0:T(8,128)(2,1)} copy(bf16[2,4,128,4096]{2,3,1,0:T(8,128)(2,1)} %bitcast.149) | data formatting | bytes 16777216 | tf_op jit(solution)/shard_map/all_to_all | solution.py:101
  481.3 1.7 slice.58
  483.0 3.7 collective-permute-start
  486.8 6.5 %cosine_convert_fusion.2.clone.5 = bf16[640,640]{1,0:T(8,128)(2,1)S(1)} fusion(), kind=kLoop, calls=%fused_computation.85.clone.clone.clone.clone.2 | loop fusion | flops 4096000 | bytes 819200 | tf_op jit(solution)/shard_map/convert_element_type | solution.py:26
  493.4 2.3 compare_or_fusion
  495.7 15.8 %collective-permute-done = bf16[2,128,4096]{2,1,0:T(8,128)(2,1)S(1)} collective-permute-done((bf16[2,128,4096]{2,1,0:T(8,128)(2,1)S(1)}, bf16[2,128,4096]{2,1,0:T(8,128)(2,1)S(1)}, u32[]{:S(2)}, u32[]{:S(2)}) %collective-permute-start) | collective-permute-done | bytes 2097184 | tf_op jit(solution)/shard_map/ppermute | solution.py:14
  511.6 7.9 %maximum_select_fusion = bf16[2,640,4096]{2,1,0:T(8,128)(2,1)S(1)} fusion(bf16[2,128,4096]{2,1,0:T(8,128)(2,1)S(1)} %collective-permute-done, bf16[2,512,4096]{2,1,0:T(8,128)(2,1)} %bitcast.140, pred[640,4096]{1,0:T(8,128)(4,1)S(1)} %compare_or_fusion), kind=kLoop, calls=%fused_computation.23 | loop fusion | flops 26214400 | bytes 23592960 | tf_op jit(solution)/shard_map/jit(_where)/select_n | solution.py:108
  519.5 12.6 %fusion.40 = f32[640,4096]{1,0:T(8,128)} fusion(bf16[2,640,4096]{2,1,0:T(8,128)(2,1)S(1)} %maximum_select_fusion), kind=kOutput, calls=%fused_computation.62 | convolution fusion | flops 3359539200 | bytes 15728640 | tf_op jit(solution)/shard_map/fp,pr->fr/dot_general | solution.py:34
  532.1 12.9 %fusion.39 = f32[640,4096]{1,0:T(8,128)} fusion(bf16[2,640,4096]{2,1,0:T(8,128)(2,1)S(1)} %maximum_select_fusion), kind=kOutput, calls=%fused_computation.61 | convolution fusion | flops 3359539200 | bytes 15728640 | tf_op jit(solution)/shard_map/fp,pr->fr/dot_general | solution.py:37
  545.0 12.9 %convolution_subtract_fusion = f32[640,4096]{1,0:T(8,128)S(1)} fusion(f32[640,4096]{1,0:T(8,128)} %fusion.40, bf16[2,640,4096]{2,1,0:T(8,128)(2,1)S(1)} %maximum_select_fusion), kind=kOutput, calls=%fused_computation.58 | convolution fusion | flops 3362160640 | bytes 26214400 | tf_op jit(solution)/shard_map/fp,pr->fr/dot_general | solution.py:32
  557.9 46.4 %subtract_convert_fusion = (bf16[640,4096]{1,0:T(8,128)(2,1)S(1)}, bf16[640,4096]{1,0:T(8,128)(2,1)}) fusion(f32[640,4096]{1,0:T(8,128)S(1)} %convolution_subtract_fusion, f32[640]{0:T(1024)S(1)} %fusion.111, f32[4096]{0:T(1024)S(1)} %broadcast_multiply_fusion, f32[640,4096]{1,0:T(8,128)} %fusion.39, bf16[2,640,4096]{2,1,0:T(8,128)(2,1)S(1)} %maximum_select_fusion, ...), kind=kOutput, calls=%fused_computation.25 | convolution fusion | flops 3386900480 | bytes 37539840 | tf_op jit(solution)/shard_map/fp,pr->fr/dot_general | solution.py:35
  604.4 0.0 slice-start
  604.4 0.0 slice-start.1
  604.4 8.0 %fusion.63 = f32[512,4096]{1,0:T(8,128)S(1)} fusion(bf16[640,4096]{1,0:T(8,128)(2,1)S(1)} %get-tuple-element.21), kind=kOutput, calls=%fused_computation.99 | convolution fusion | flops 2687631360 | bytes 13631488 | tf_op jit(solution)/shard_map/qf,fr->qr/dot_general | solution.py:32
  612.4 0.0 copy-done.8
  612.4 0.0 slice-done
  612.4 0.0 slice-done.1
  612.4 8.4 %fusion.62 = f32[512,4096]{1,0:T(8,128)S(1)} fusion(bf16[640,4096]{1,0:T(8,128)(2,1)S(1)} %bitcast.159), kind=kOutput, calls=%fused_computation.98 | convolution fusion | flops 2687631360 | bytes 13631488 | tf_op jit(solution)/shard_map/qf,fr->qr/dot_general | solution.py:35
  620.9 0.0 copy-start.9
  620.9 8.1 %subtract_bitcast_fusion = f32[1,1,512,4096]{3,2,1,0:T(8,128)S(1)} fusion(f32[512,4096]{1,0:T(8,128)S(1)} %fusion.63, bf16[640,4096]{1,0:T(8,128)(2,1)S(1)} %bitcast.159), kind=kOutput, calls=%fused_computation.41 | convolution fusion | flops 2689728512 | bytes 22020096 | tf_op jit(solution)/shard_map/qf,fr->qr/dot_general | solution.py:34
  629.0 0.0 copy-done.9
  629.0 8.3 %add_bitcast_fusion = f32[1,1,512,4096]{3,2,1,0:T(8,128)S(1)} fusion(f32[512,4096]{1,0:T(8,128)S(1)} %fusion.62, bf16[640,4096]{1,0:T(8,128)(2,1)S(1)} %copy-done.9), kind=kOutput, calls=%fused_computation.40 | convolution fusion | flops 2689728512 | bytes 22020096 | tf_op jit(solution)/shard_map/qf,fr->qr/dot_general | solution.py:37
  637.2 4.1 fusion.2
  (23 shorter events, 0.1 us)
Async XLA Ops:
  31.5 9.6 %copy-start = (bf16[128,128,128]{2,1,0:T(8,128)(2,1)}, bf16[128,128,128]{2,1,0:T(8,128)(2,1)S(1)}, u32[]{:S(2)}) copy-start(bf16[128,128,128]{2,1,0:T(8,128)(2,1)S(1)} %get-tuple-element.20) | copy-start | bytes 12582916
  41.1 4.7 copy-start.4
  86.7 4.9 copy-start.1
  153.9 8.2 %copy-start.2 = (bf16[2,128,128,128]{2,3,1,0:T(8,128)(2,1)S(1)}, bf16[2,128,128,128]{2,3,1,0:T(8,128)(2,1)}, u32[]{:S(2)}) copy-start(bf16[2,128,128,128]{2,3,1,0:T(8,128)(2,1)} %copy.43) | copy-start | bytes 25165828
  168.7 23.7 %copy-start.5 = (s32[16384]{0:T(1024)S(1)}, s32[16384]{0:T(1024)}, u32[]{:S(2)}) copy-start(s32[16384]{0:T(1024)} %param.8) | copy-start | bytes 196612
  168.7 23.8 %copy-start.3 = (bf16[8,16384]{1,0:T(8,128)(2,1)S(1)}, bf16[8,16384]{1,0:T(8,128)(2,1)}, u32[]{:S(2)}) copy-start(bf16[8,16384]{1,0:T(8,128)(2,1)} %param.9) | copy-start | bytes 786436
  469.2 24.2 %copy-start.7 = (f32[4096]{0:T(1024)S(1)}, f32[4096]{0:T(1024)}, u32[]{:S(2)}) copy-start(f32[4096]{0:T(1024)} %param.11) | copy-start | bytes 49156
  469.2 24.2 %copy-start.6 = (s32[4096]{0:T(1024)S(1)}, s32[4096]{0:T(1024)}, u32[]{:S(2)}) copy-start(s32[4096]{0:T(1024)} %param.10) | copy-start | bytes 49156
  483.0 28.5 %collective-permute-start = (bf16[2,128,4096]{2,1,0:T(8,128)(2,1)S(1)}, bf16[2,128,4096]{2,1,0:T(8,128)(2,1)S(1)}, u32[]{:S(2)}, u32[]{:S(2)}) collective-permute-start(bf16[2,128,4096]{2,1,0:T(8,128)(2,1)S(1)} %slice.58), channel_id=1, source_target_pairs={{1,0},{2,1},{3,2},{5,4},{6,5},{7,6},{9,8},{10,9},{11,10},{13,12},{... | collective-permute-start | bytes 6291464 | tf_op jit(solution)/shard_map/ppermute | solution.py:14
  604.3 8.1 %copy-start.8 = (bf16[640,4096]{1,0:T(8,128)(2,1)}, bf16[640,4096]{1,0:T(8,128)(2,1)S(1)}, u32[]{:S(2)}) copy-start(bf16[640,4096]{1,0:T(8,128)(2,1)S(1)} %get-tuple-element.21) | copy-start | bytes 15728644
  604.4 8.1 %slice-start = ((s8[5242880]{0:T(1024)(128)(4,1)}), s8[4194304]{0:T(1024)(128)(4,1)S(1)}, s32[]{:S(2)}) async-start(s8[5242880]{0:T(1024)(128)(4,1)} %bitcast.158), calls=%async_computation.1 | async-start | bytes 8388608
  604.4 8.1 %slice-start.1 = ((s8[5242880]{0:T(1024)(128)(4,1)}), s8[1048576]{0:T(1024)(128)(4,1)S(1)}, s32[]{:S(2)}) async-start(s8[5242880]{0:T(1024)(128)(4,1)} %bitcast.158), calls=%async_computation.2 | async-start | bytes 2097152
  620.9 8.1 %copy-start.9 = (bf16[640,4096]{1,0:T(8,128)(2,1)S(1)}, bf16[640,4096]{1,0:T(8,128)(2,1)}, u32[]{:S(2)}) copy-start(bf16[640,4096]{1,0:T(8,128)(2,1)} %copy-done.8) | copy-start | bytes 15728644
where the time goes:
time: 649 us; the launch traced here: 642 us
  matrix products  234 us (36%)
  blocking collectives  187 us (29%)
  local copies, waits for them, and re-layouts  119 us (18%)
  other arithmetic  80.3 us (12%)
  waiting for transfers between devices  15.8 us (2%)
    all_to_all x1, blocking collectives, shards(): lax.all_to_all(outgoing, 'bins', split_axis=2, concat_axis=1, tiled=True)  187 us
    dot_general x6, matrix products, complex_product(): jnp.einsum(form, left_real, right_imag, preferred_element_type=jnp.float32)  93.1 us
    dot_general x6, matrix products, complex_product(): jnp.einsum(form, left_real, right_real, preferred_element_type=jnp.float32)  51.5 us
    dot_general x6, matrix products, complex_product(): jnp.einsum(form, left_imag, right_imag, preferred_element_type=jnp.float32)  39.7 us
    dot_general x1, other arithmetic, migrate(): jnp.einsum('sprj,rjk->sprk', windows, band_matrix, preferred_element_type...  38.2 us
    dot_general x6, matrix products, complex_product(): jnp.einsum(form, left_imag, right_real, preferred_element_type=jnp.float32)  37.1 us
    convert_element_type x2, local copies, waits for them, and re-layouts, migrate(): return result.reshape(2, row_count, line_width).astype(jnp.bfloat16)  26.1 us
    concatenate x1, local copies, waits for them, and re-layouts, migrate(): jnp.concatenate([extended[:, :, :line_width].reshape(2, row_count, blocks...  23.6 us
  transfers between devices with their start and end apart: 1, of which 1 were waited for; matrix products, arithmetic and copies ran while one was open for 1% of the time, Pallas kernels for 0%

commit v1 on v0

v1 whole, which is shorter than its diff:
```python
import functools
import math

import jax
import jax.numpy as jnp
import ml_dtypes
import numpy as np
from jax import lax
from jax.experimental import pallas as pl
from jax.experimental.pallas import tpu as pltpu
from jax.sharding import PartitionSpec as P

OVLMAX = 128
LANES = 128
SLAB = 16
VMEM_BYTES = 60 * 1024 * 1024


def fit_turns(power_start, terms):
    grid = 0.5 * np.cos(np.pi * (np.arange(4001) + 0.5) / 4001)
    basis = np.stack([grid ** (power_start + 2 * i) for i in range(terms)], axis=1)
    target = np.sin(2 * np.pi * grid) if power_start else np.cos(2 * np.pi * grid)
    return [float(c) for c in np.linalg.lstsq(basis, target, rcond=None)[0]]


SIN_TERMS = fit_turns(1, 7)
COS_TERMS = fit_turns(0, 7)


def turn_pair(turns):
    rest = turns - jnp.round(turns)
    square = rest * rest
    cosine = jnp.full_like(square, COS_TERMS[-1])
    sine = jnp.full_like(square, SIN_TERMS[-1])
    for c in COS_TERMS[-2::-1]:
        cosine = cosine * square + c
    for c in SIN_TERMS[-2::-1]:
        sine = sine * square + c
    return cosine, sine * rest


def unit_roots(rows, cols, length):
    angle = 2.0 * np.pi * (np.multiply.outer(rows, cols) % length) / length
    return np.cos(angle), np.sin(angle)


def left_table(cosine, sine, sign, scale=1.0):
    table = np.block([[cosine, -sign * sine], [sign * sine, cosine]]) * scale
    return table.astype(ml_dtypes.bfloat16)


def right_table(cosine, sine, sign, scale=1.0):
    table = np.block([[cosine, sign * sine], [-sign * sine, cosine]]) * scale
    return table.astype(ml_dtypes.bfloat16)


def dot(left, right):
    return jnp.dot(left, right, preferred_element_type=jnp.float32)


def range_kernel(plan, z_ref, raw_ref, phase_ref, starts_ref, weights_ref, twiddle_ref, first_ref, second_ref, third_ref, last_ref, *rest):
    first_pulse, pulses, bin_count, group_tiles, pair = plan
    out_refs = rest[: bin_count * len(group_tiles)]
    raw_v, slab_v, comp_v, filter_v, sems = rest[bin_count * len(group_tiles) :]
    heights = raw_ref.shape[-1] // LANES
    slabs = pulses // SLAB
    copies = [
        pltpu.make_async_copy(
            raw_ref.at[:, 0, pl.ds(first_pulse + SLAB * s, SLAB), :],
            raw_v.at[:, pl.ds(SLAB * s, SLAB), :],
            sems.at[s],
        )
        for s in range(slabs)
    ]
    for copy in copies:
        copy.start()
    cosine, sine = turn_pair(phase_ref[...].T * (0.5 / math.pi))
    filter_v[0] = cosine
    filter_v[1] = sine
    stride = comp_v.shape[0] // (heights + 1)
    comp_v[pl.ds(heights * stride, stride), :] = jnp.zeros((stride, LANES), jnp.float32)

    def slab_step(s, carry):
        row = pl.multiple_of(s * SLAB, SLAB)
        pltpu.make_async_copy(
            raw_ref.at[:, 0, pl.ds(pl.multiple_of(first_pulse + row, SLAB), SLAB), :],
            raw_v.at[:, pl.ds(row, SLAB), :],
            sems.at[s],
        ).wait()
        for comp in range(2):
            for a in range(heights):
                tile = raw_v[comp, pl.ds(row, SLAB), pl.ds(a * LANES, LANES)]
                slab_v[pl.ds((comp * heights + a) * SLAB, SLAB), :] = tile.astype(jnp.float32)

        def pulse_step(j, inner):
            columns = [
                slab_v[pl.ds(j * pair + i, 2 * heights, stride=SLAB), :].astype(jnp.bfloat16)
                for i in range(pair)
            ]
            part = dot(first_ref[...], jnp.concatenate(columns, axis=1))
            tw_cos, tw_sin = twiddle_ref[0], twiddle_ref[1]
            rows = []
            for i in range(pair):
                real = part[:heights, i * LANES : (i + 1) * LANES]
                imag = part[heights:, i * LANES : (i + 1) * LANES]
                rows.append(
                    jnp.concatenate(
                        [
                            (real * tw_cos + imag * tw_sin).astype(jnp.bfloat16),
                            (imag * tw_cos - real * tw_sin).astype(jnp.bfloat16),
                        ],
                        axis=1,
                    )
                )
            spectrum = dot(jnp.concatenate(rows, axis=0), second_ref[...])
            f_cos, f_sin = filter_v[0], filter_v[1]
            rows = []
            for i in range(pair):
                real = spectrum[i * heights : (i + 1) * heights, :LANES]
                imag = spectrum[i * heights : (i + 1) * heights, LANES:]
                rows.append(
                    jnp.concatenate(
                        [
                            (real * f_cos + imag * f_sin).astype(jnp.bfloat16),
                            (imag * f_cos - real * f_sin).astype(jnp.bfloat16),
                        ],
                        axis=1,
                    )
                )
            part = dot(jnp.concatenate(rows, axis=0), third_ref[...])
            columns = []
            for i in range(pair):
                real = part[i * heights : (i + 1) * heights, :LANES]
                imag = part[i * heights : (i + 1) * heights, LANES:]
                columns.append(
                    jnp.concatenate(
                        [
                            (real * tw_cos - imag * tw_sin).astype(jnp.bfloat16),
                            (imag * tw_cos + real * tw_sin).astype(jnp.bfloat16),
                        ],
                        axis=0,
                    )
                )
            line = dot(last_ref[...], jnp.concatenate(columns, axis=1))
            for i in range(pair):
                pulse = s * SLAB + j * pair + i
                for comp in range(2):
                    comp_v[pl.ds(comp * pulses + pulse, heights, stride=stride), :] = line[
                        comp * heights : (comp + 1) * heights, i * LANES : (i + 1) * LANES
                    ]
            return inner

        lax.fori_loop(0, SLAB // pair, pulse_step, 0)
        return carry

    lax.fori_loop(0, slabs, slab_step, 0)

    z = z_ref[0]
    tiles_per_device = heights // bin_count
    sub = lax.broadcasted_iota(jnp.int32, (8, LANES), 0)
    step = 0
    for mask in range(bin_count):
        tile_base = lax.bitwise_xor(z, mask) * tiles_per_device
        group_base = 0
        for group, tiles in enumerate(group_tiles):
            out_ref = out_refs[group * bin_count + mask]

            def migrate_step(t, carry, tile_base=tile_base, group_base=group_base, out_ref=out_ref):
                r = tile_base + group_base + t
                lane = pl.multiple_of(r * LANES, LANES)
                offset = starts_ref[pl.ds(r, 1), :] - lane
                low = lax.bitwise_and(offset, 7)
                taps = weights_ref[:, pl.ds(lane, LANES)].astype(jnp.float32)
                turned = lax.bitwise_and(sub - low, 7)
                weight = jnp.zeros((8, LANES), jnp.float32)
                for tap in range(8):
                    weight = jnp.where(turned == tap, taps[tap : tap + 1, :], weight)
                where_tile = lax.shift_right_logical(offset, 3) + jnp.where(sub < low, 1, 0)
                zero = jnp.zeros((8, LANES), jnp.float32)
                band = [
                    jnp.where(where_tile == i, weight, zero) if i < 26 else zero for i in range(2 * LANES // 8)
                ]
                band = jnp.concatenate(band, axis=0).astype(jnp.bfloat16)
                base = pl.multiple_of(r * stride, 8)
                window = jnp.concatenate(
                    [
                        comp_v[pl.ds(base, 2 * pulses), :].astype(jnp.bfloat16),
                        comp_v[pl.ds(base + stride, 2 * pulses), :].astype(jnp.bfloat16),
                    ],
                    axis=1,
                )
                value = dot(window, band).astype(jnp.bfloat16)
                at = pl.multiple_of(t * LANES, LANES)
                out_ref[0, :, pl.ds(at, LANES)] = value[:pulses]
                out_ref[1, :, pl.ds(at, LANES)] = value[pulses:]
                return carry

            lax.fori_loop(0, tiles, migrate_step, 0)
            group_base += tiles


def range_call(z, raw, phase, starts, weights, tables, first_pulse, pulses, bin_count, group_tiles):
    heights = raw.shape[-1] // LANES
    pair = 4
    stride = 2 * pulses + 8
    plan = (first_pulse, pulses, bin_count, tuple(group_tiles), pair)
    vmem = pl.BlockSpec(memory_space=pltpu.VMEM)
    return pl.pallas_call(
        functools.partial(range_kernel, plan),
        out_shape=[
            jax.ShapeDtypeStruct((2, pulses, tiles * LANES), jnp.bfloat16)
            for tiles in group_tiles
            for _ in range(bin_count)
        ],
        in_specs=[pl.BlockSpec(memory_space=pltpu.SMEM), pl.BlockSpec(memory_space=pl.ANY)] + [vmem] * (3 + len(tables)),
        out_specs=[vmem] * (bin_count * len(group_tiles)),
        scratch_shapes=[
            pltpu.VMEM((2, pulses, raw.shape[-1]), jnp.bfloat16),
            pltpu.VMEM((2 * heights * SLAB, LANES), jnp.float32),
            pltpu.VMEM(((heights + 1) * stride, LANES), jnp.float32),
            pltpu.VMEM((2, heights, LANES), jnp.float32),
            pltpu.SemaphoreType.DMA((pulses // SLAB,)),
        ],
        compiler_params=pltpu.CompilerParams(vmem_limit_bytes=VMEM_BYTES),
        cost_estimate=pl.CostEstimate(
            flops=90 * 10**6 * pulses, bytes_accessed=2 * 4 * pulses * raw.shape[-1], transcendentals=0
        ),
        name="range_lines",
    )(z, raw, phase, starts, weights, *tables)


def range_tables(width):
    heights = width // LANES
    first = unit_roots(np.arange(heights), np.arange(heights), heights)
    second = unit_roots(np.arange(LANES), np.arange(LANES), LANES)
    twiddle = np.stack(unit_roots(np.arange(heights), np.arange(LANES), width)).astype(np.float32)
    return (
        twiddle,
        left_table(*first, -1.0),
        right_table(*second, -1.0),
        right_table(*second, 1.0, 1.0 / LANES),
        left_table(*first, 1.0, 1.0 / heights),
    )


def head_kernel(sources, masks, z_ref, *rest):
    in_refs, out_ref, sem = rest[:masks], rest[masks], rest[masks + 1]
    z = z_ref[0]
    for source in range(sources):
        wanted = lax.bitwise_xor(z, source)
        for mask in range(masks):

            @pl.when(wanted == mask)
            def _(mask=mask, source=source):
                pltpu.make_async_copy(in_refs[mask], out_ref.at[source], sem.at[source]).start()

    for source in range(sources):
        pltpu.make_async_copy(in_refs[0], out_ref.at[source], sem.at[source]).wait()


def pick_head(z, pieces, sources):
    shape = pieces[0].shape
    return pl.pallas_call(
        functools.partial(head_kernel, sources, len(pieces)),
        out_shape=jax.ShapeDtypeStruct((sources,) + shape, jnp.bfloat16),
        in_specs=[pl.BlockSpec(memory_space=pltpu.SMEM)] + [pl.BlockSpec(memory_space=pl.ANY)] * len(pieces),
        out_specs=pl.BlockSpec(memory_space=pl.ANY),
        scratch_shapes=[pltpu.SemaphoreType.DMA((sources,))],
        compiler_params=pltpu.CompilerParams(vmem_limit_bytes=VMEM_BYTES),
        name="pick_head",
    )(z, *pieces)


def azimuth_kernel(plan, z_ref, length_ref, rate_ref, forward_ref, inverse_ref, *rest):
    parts, device_pulses, bin_count, lane_offset, width, tile, chained = plan
    count = len(parts) * (bin_count + 1)
    piece_refs = rest[:count]
    rest = rest[count + (1 if chained else 0) :]
    image_ref, aperture_v, spectrum_v, narrow_v, image_v, sems, out_sem = rest
    z = z_ref[0]
    lines = image_ref.shape[2]
    length = aperture_v.shape[1]
    half = length // 2
    copies = []
    at = 0
    for start, pulses, from_lane in parts:
        lanes = pl.ds(from_lane, width)
        for mask in range(bin_count):
            source = lax.bitwise_xor(z, mask)
            row = pl.multiple_of(source * device_pulses + start, SLAB)
            copies.append(
                pltpu.make_async_copy(
                    piece_refs[at].at[:, :, lanes], aperture_v.at[:, pl.ds(row, pulses), :], sems.at[len(copies)]
                )
            )
            at += 1
        heads = piece_refs[at]
        at += 1
        for source in range(heads.shape[0]):
            row = lines + source * device_pulses + start
            copies.append(
                pltpu.make_async_copy(
                    heads.at[source, :, :, lanes], aperture_v.at[:, pl.ds(row, pulses), :], sems.at[len(copies)]
                )
            )
    for copy in copies:
        copy.start()
    for copy in copies:
        copy.wait()

    block = 64
    for lane in range(0, width, tile):
        lanes = pl.ds(lane, tile)
        reach = length_ref[:, lanes]
        for row in range(lines, length, SLAB):
            pulse = lax.broadcasted_iota(jnp.int32, (SLAB, tile), 0) + (row - lines)
            inside = pulse < reach
            for comp in range(2):
                held = aperture_v[comp, pl.ds(row, SLAB), lanes].astype(jnp.float32)
                aperture_v[comp, pl.ds(row, SLAB), lanes] = jnp.where(inside, held, 0.0).astype(jnp.bfloat16)
        aperture = jnp.concatenate([aperture_v[0, :, lanes], aperture_v[1, :, lanes]], axis=0)
        spectrum_v[...] = dot(forward_ref[...], aperture)
        rate = rate_ref[:, lanes]

        def filter_rows(cosine, sine, row, size):
            real = spectrum_v[pl.ds(row, size), :]
            imag = spectrum_v[pl.ds(length + row, size), :]
            narrow_v[pl.ds(row, size), :] = (real * cosine + imag * sine).astype(jnp.bfloat16)
            narrow_v[pl.ds(length + row, size), :] = (imag * cosine - real * sine).astype(jnp.bfloat16)

        def filter_step(j, carry):
            row = pl.multiple_of(j * block, block)
            doppler = (lax.broadcasted_iota(jnp.int32, (block, tile), 0) + row).astype(jnp.float32)
            cosine, sine = turn_pair(rate * (doppler * doppler * (0.5 / length)))
            filter_rows(cosine, sine, row, block)
            doppler = jnp.where(doppler == 0.0, float(half), doppler)
            cosine, sine = turn_pair(rate * (doppler * doppler * (0.5 / length)))
            filter_rows(cosine, sine, pl.multiple_of(half + row, block), block)
            return carry

        lax.fori_loop(0, half // block, filter_step, 0)
        image = dot(inverse_ref[...], narrow_v[...]) * (1.0 / length)
        image_v[0, :, lanes] = image[:lines].astype(jnp.bfloat16)
        image_v[1, :, lanes] = image[lines:].astype(jnp.bfloat16)
    out = pltpu.make_async_copy(image_v, image_ref.at[:, 0, :, pl.ds(lane_offset, width)], out_sem)
    out.start()
    out.wait()


def azimuth_call(z, lengths, rates, tables, pieces, parts, device_pulses, bin_count, lane_offset, width, image_shape, image):
    vmem = pl.BlockSpec(memory_space=pltpu.VMEM)
    lines = image_shape[2]
    length = lines + OVLMAX
    tile = 2 * LANES if width % (2 * LANES) == 0 else LANES
    chained = image is not None
    plan = (tuple(parts), device_pulses, bin_count, lane_offset, width, tile, chained)
    sources = pieces[bin_count].shape[0]
    lengths = lax.slice_in_dim(lengths, lane_offset, lane_offset + width)[None]
    rates = lax.slice_in_dim(rates, lane_offset, lane_offset + width)[None]
    operands = [z, lengths, rates, *tables, *pieces] + ([image] if chained else [])
    any_spec = pl.BlockSpec(memory_space=pl.ANY)
    return pl.pallas_call(
        functools.partial(azimuth_kernel, plan),
        out_shape=jax.ShapeDtypeStruct(image_shape, jnp.bfloat16),
        in_specs=[pl.BlockSpec(memory_space=pltpu.SMEM)] + [vmem] * 4 + [any_spec] * (len(operands) - 5),
        out_specs=any_spec,
        scratch_shapes=[
            pltpu.VMEM((2, length, width), jnp.bfloat16),
            pltpu.VMEM((2 * length, tile), jnp.float32),
            pltpu.VMEM((2 * length, tile), jnp.bfloat16),
            pltpu.VMEM((2, lines, width), jnp.bfloat16),
            pltpu.SemaphoreType.DMA((len(parts) * (bin_count + sources),)),
            pltpu.SemaphoreType.DMA,
        ],
        input_output_aliases={len(operands) - 1: 0} if chained else {},
        compiler_params=pltpu.CompilerParams(vmem_limit_bytes=VMEM_BYTES),
        cost_estimate=pl.CostEstimate(
            flops=2 * width * (2 * length) * (2 * length + 2 * lines),
            bytes_accessed=4 * (2 * lines + OVLMAX) * width,
            transcendentals=0,
        ),
        name="azimuth_bins",
    )(*operands)


def azimuth_tables(lines):
    length = lines + OVLMAX
    half = length // 2
    order = np.concatenate([np.arange(half), [half], length - np.arange(1, half)])
    forward = left_table(*unit_roots(order, np.arange(length), length), -1.0)
    inverse = left_table(*unit_roots(np.arange(lines), order, length), 1.0)
    return forward, inverse


def exchanged(value, mask):
    count = lax.axis_size("bins")
    return lax.ppermute(value, "bins", [(s, s ^ mask) for s in range(count)]) if mask else value


def passed_back(value):
    count = lax.axis_size("az")
    return lax.ppermute(value, "az", [(s, s - 1) for s in range(1, count)])


def split_tiles(tiles):
    small = max(1, tiles // 8)
    big = max(1, (tiles - 2 * small) // 2)
    shares = []
    while sum(shares) + big + 2 * small <= tiles:
        shares.append(big)
    rest = tiles - sum(shares) - 2 * small
    if rest > 0:
        shares.append(rest)
    return shares + [small, small]


def shards(raw_echoes, range_phase, band_start, band_weight, intersection_length, azimuth_rate):
    bin_count = lax.axis_size("bins")
    width = raw_echoes.shape[-1]
    heights = width // LANES
    device_pulses = raw_echoes.shape[2]
    lines = device_pulses * bin_count
    device_bins = width // bin_count
    device_tiles = device_bins // LANES
    z = lax.axis_index("bins").astype(jnp.int32).reshape(1)
    phase = range_phase.reshape(LANES, heights)
    starts = band_start.reshape(heights, LANES)
    tables = [jnp.asarray(t) for t in range_tables(width)]
    sources = max(1, OVLMAX // device_pulses)
    first = max(SLAB, device_pulses // 4 // SLAB * SLAB)
    shares = split_tiles(device_tiles)

    def line_call(at, pulses, tiles):
        return range_call(z, raw_echoes, phase, starts, band_weight, tables, at, pulses, bin_count, tiles)

    early = line_call(0, first, [device_tiles])
    early = [exchanged(v, m) for m, v in enumerate(early)]
    late = line_call(first, device_pulses - first, shares)
    early_head = passed_back(pick_head(z, early, sources))
    late = [
        [exchanged(v, m) for m, v in enumerate(late[g * bin_count : (g + 1) * bin_count])] for g in range(len(shares))
    ]
    late_heads = [passed_back(pick_head(z, pieces, sources)) for pieces in late]
    az_tables = [jnp.asarray(t) for t in azimuth_tables(lines)]
    image_shape = (2, 1, lines, device_bins)
    image = None
    offset = 0
    for share, pieces, head in zip(shares, late, late_heads):
        image = azimuth_call(
            z,
            intersection_length,
            azimuth_rate,
            az_tables,
            [*early, early_head, *pieces, head],
            [(0, first, offset), (first, device_pulses - first, 0)],
            device_pulses,
            bin_count,
            offset,
            share * LANES,
            image_shape,
            image,
        )
        offset += share * LANES
    return image


def solution(mesh):
    in_specs = (P(None, ("scene", "az"), "bins", None), P(), P(), P(), P("bins"), P("bins"))
    out_specs = P(None, ("scene", "az"), None, "bins")
    return jax.shard_map(shards, mesh=mesh, in_specs=in_specs, out_specs=out_specs, check_vma=False)
```

time: 649 us -> 401 us (0.62)
  Pallas kernels: 0 us -> 240 us
  matrix products: 234 us -> 0 us
  blocking collectives: 187 us -> 0 us
  local copies, waits for them, and re-layouts: 119 us -> 9.1 us
  other arithmetic: 80.3 us -> 0 us
  waiting for transfers between devices: 15.8 us -> 83.8 us
  starting transfers between devices: 3.72 us -> 61.5 us
    pallas_call x0 -> x11, Pallas kernels: none -> 240 us  [the longest x4 90.1 us: azimuth_call(): pl.pallas_call(functools.partial(azimuth_kernel, plan), out_shape=jax.Sha...]
    dot_general x25 -> x0, matrix products: 234 us -> none  [the longest x6 93.1 us: complex_product(): jnp.einsum(form, left_real, right_imag, preferred_element_type=jnp.float32)]
    all_to_all x1 -> x0, blocking collectives: 187 us -> none  [shards(): lax.all_to_all(outgoing, 'bins', split_axis=2, concat_axis=1, tiled=True)]
    ppermute x1 -> x20, waiting for transfers between devices: 15.8 us -> 83.8 us  [the longest x15 83.7 us: exchanged(): lax.ppermute(value, 'bins', [(s, s ^ mask) for s in range(count)])]
    ppermute x1 -> x20, starting transfers between devices: 3.72 us -> 61.5 us  [the longest x15 33.9 us: exchanged(): lax.ppermute(value, 'bins', [(s, s ^ mask) for s in range(count)])]
    dot_general x1 -> x0, other arithmetic: 38.2 us -> none  [migrate(): jnp.einsum('sprj,rjk->sprk', windows, band_matrix, preferred_element_type...]
    convert_element_type x2 -> x0, local copies, waits for them, and re-layouts: 26.1 us -> none  [migrate(): return result.reshape(2, row_count, line_width).astype(jnp.bfloat16)]
    convert_element_type x4 -> x0, other arithmetic: 24.4 us -> none  [the longest x2 13.8 us: compress_lines(): return stacked.reshape(2, line_count, line_width).astype(jnp.bfloat16)]
  transfers between devices with their start and end apart: 1 -> 20, of which waited for: 1 -> 2; matrix products, arithmetic and copies ran while one was open for 1% -> 1% of each run, Pallas kernels for 0% -> 49%
where the time goes in v1:
time: 401 us; the launch traced here: 395 us
  Pallas kernels  240 us (60%)
  waiting for transfers between devices  83.8 us (21%)
  starting transfers between devices  61.5 us (15%)
  local copies, waits for them, and re-layouts  9.1 us (2%)
    pallas_call x4, Pallas kernels, azimuth_call(): pl.pallas_call(functools.partial(azimuth_kernel, plan), out_shape=jax.Sha...  90.1 us
    ppermute x15, waiting for transfers between devices, exchanged(): lax.ppermute(value, 'bins', [(s, s ^ mask) for s in range(count)])  83.7 us
    pallas_call x2, Pallas kernels, range_call(): pl.pallas_call(functools.partial(range_kernel, plan), out_shape=[jax.Shap...  80.9 us
    pallas_call x5, Pallas kernels, pick_head(): pl.pallas_call(functools.partial(head_kernel, sources, len(pieces)), out_...  69.1 us
    ppermute x15, starting transfers between devices, exchanged(): lax.ppermute(value, 'bins', [(s, s ^ mask) for s in range(count)])  33.9 us
    ppermute x5, starting transfers between devices, passed_back(): return lax.ppermute(value, 'az', [(s, s - 1) for s in range(1, count)])  27.6 us
  transfers between devices with their start and end apart: 20, of which 2 were waited for; matrix products, arithmetic and copies ran while one was open for 1% of the time, Pallas kernels for 49%

profile of v1, /device:TPU:1, one launch (start us, length us, event | category | flops | bytes accessed | tf_op | source)
XLA Modules:
  0.0 395.0 jit_solution(8499021767816138518)
XLA Ops:
  0.0 31.2 %range_lines.2 = (bf16[2,32,4096]{2,1,0:T(8,128)(2,1)}, bf16[2,32,4096]{2,1,0:T(8,128)(2,1)}, bf16[2,32,4096]{2,1,0:T(8,128)(2,1)}, bf16[2,32,4096]{2,1,0:T(8,128)(2,1)}) custom-call(s32[1]{0:T(128)} %bitcast.z_ref, bf16[2,1,128,16384]{3,2,1,0:T(8,128)(2,1)} %raw_ref.3, f32[128,128]{1,0:T(8,128)} %bitcast.11, s32[128,128]{1,0:T(8,128)} %bitcast.13, ...), custom_call_target="tpu_custom_call" | custom-call | flops 2880000000 | bytes 4194304 | tf_op jit(solution)/shard_map/range_lines/pallas_call | solution.py:208
  31.2 0.0 copy-start.18
  31.2 0.0 copy-start.19
  31.3 2.2 collective-permute-start
  33.5 49.7 %range_lines.3 = (bf16[2,96,1536]{2,1,0:T(8,128)(2,1)}, bf16[2,96,1536]{2,1,0:T(8,128)(2,1)}, bf16[2,96,1536]{2,1,0:T(8,128)(2,1)}, bf16[2,96,1536]{2,1,0:T(8,12...) custom-call(s32[1]{0:T(128)} %bitcast.z_ref, ...), custom_call_target="tpu_custom_call" | custom-call | flops 8640000000 | bytes 12582912 | tf_op jit(solution)/shard_map/range_lines/pallas_call | solution.py:208
  83.1 2.2 collective-permute-start.10
  85.4 0.4 collective-permute-start.16
  85.8 1.0 collective-permute-start.17
  86.8 2.2 collective-permute-start.18
  88.9 1.8 collective-permute-done.10.rest_3_.rest_8_
  90.8 5.1 %collective-permute-start.1 = (bf16[2,32,4096]{2,1,0:T(8,128)(2,1)}, bf16[2,32,4096]{2,1,0:T(8,128)(2,1)S(1)}, u32[]{:S(2)}, u32[]{:S(2)}) collective-permute-start(bf16[2,32,4096]{2,1,0:T(8,128)(2,1)} %get-tuple-element.27), channel_id=1, source_target_pairs={{0,8},{4,12},{8,0},{12,4},{1,9},{5,13},{9,1},{13,5},{2,10},{6,14},... | collective-permute-start | bytes 1572872 | tf_op jit(solution)/shard_map/ppermute | solution.py:397
  95.9 0.0 collective-permute-done.rest_1_
  95.9 0.8 collective-permute-start.2
  96.8 81.9 %collective-permute-done.1.rest_2_ = bf16[2,32,4096]{2,1,0:T(8,128)(2,1)S(1)} collective-permute-done((bf16[2,32,4096]{2,1,0:T(8,128)(2,1)}, bf16[2,32,4096]{2,1,0:T(8,128)(2,1)S(1)}, u32[]{:S(2)}, u32[]{:S(2)}) %collective-permute-start.1) | collective-permute-done | bytes 524320 | tf_op jit(solution)/shard_map/ppermute | solution.py:397
  178.6 0.0 collective-permute-start.8
  178.6 0.0 collective-permute-done.2.rest_3_
  178.6 12.8 %collective-permute-start.9 = (bf16[2,96,512]{2,1,0:T(8,128)(2,1)}, bf16[2,96,512]{2,1,0:T(8,128)(2,1)S(1)}, u32[]{:S(2)}, u32[]{:S(2)}) collective-permute-start(bf16[2,96,512]{2,1,0:T(8,128)(2,1)} %get-tuple-element.35), channel_id=1, source_target_pairs={{0,8},{4,12},{8,0},{12,4},{1,9},{5,13},{9,1},{13,5},{2,10},{6,14},... | collective-permute-start | bytes 589832 | tf_op jit(solution)/shard_map/ppermute | solution.py:397
  191.5 0.0 collective-permute-done.16.rest_1_.rest_6_
  191.5 0.0 collective-permute-start.4
  191.5 0.0 collective-permute-done.17.rest_2_.rest_7_
  191.5 1.0 collective-permute-start.5
  192.5 0.0 collective-permute-done.18.rest_3_.rest_8_
  192.5 0.8 copy-done.12
  193.3 2.5 collective-permute-start.6
  195.9 17.0 %pick_head.5 = bf16[1,2,32,4096]{3,2,1,0:T(8,128)(2,1)} custom-call(s32[1]{0:T(128)} %bitcast.z_ref, bf16[2,32,4096]{2,1,0:T(8,128)(2,1)} %get-tuple-element.25.rest_0_, bf16[2,32,4096]{2,1,0:T(8,128)(2,1)} %copy-done, bf16[2,32,4096]{2,1,0:T(8,128)(2,1)} %copy-done.1, bf16[2,32,4096]{2,1,0:T(8,128)(2,1)} %copy-done.2), custom_call_target="tpu_custom_call" | custom-call | tf_op jit(solution)/shard_map/pick_head/pallas_call | solution.py:263
  212.9 19.0 %pick_head.9 = bf16[1,2,96,1536]{3,2,1,0:T(8,128)(2,1)} custom-call(s32[1]{0:T(128)} %bitcast.z_ref, bf16[2,96,1536]{2,1,0:T(8,128)(2,1)} %get-tuple-element.41.rest_0_.rest_5_, bf16[2,96,1536]{2,1,0:T(8,128)(2,1)} %copy-done.10, bf16[2,96,1536]{2,1,0:T(8,128)(2,1)} %copy-done.11, bf16[2,96,1536]{2,1,0:T(8,128)(2,1)} %copy-done.12), custom_call_target="tpu_custom_call" | custom-call | tf_op jit(solution)/shard_map/pick_head/pallas_call | solution.py:263
  231.9 0.0 collective-permute-done.8.rest_1_.rest_6_
  231.9 0.1 collective-permute-start.12
  232.0 0.0 collective-permute-done.9.rest_2_.rest_7_
  232.0 1.0 collective-permute-start.13
  233.0 0.0 collective-permute-done.4.rest_1_.rest_6_
  233.0 2.5 collective-permute-start.14
  235.5 0.0 collective-permute-done.5.rest_2_.rest_7_
  235.5 5.2 %collective-permute-start.3 = (bf16[1,2,32,4096]{3,2,1,0:T(8,128)(2,1)}, bf16[1,2,32,4096]{3,2,1,0:T(8,128)(2,1)S(1)}, u32[]{:S(2)}, u32[]{:S(2)}) collective-permute-start(bf16[1,2,32,4096]{3,2,1,0:T(8,128)(2,1)} %pick_head.5), channel_id=1, source_target_pairs={{1,0},{2,1},{3,2},{5,4},{6,5},{7,6},{9,8},{10,9},{11,10},{13,12},{... | collective-permute-start | bytes 1572872 | tf_op jit(solution)/shard_map/ppermute | solution.py:402
  240.7 0.0 collective-permute-done.6.rest_3_.rest_8_
  240.8 1.9 collective-permute-start.19
  242.7 0.6 broadcast_in_dim.30.length_ref
  243.3 0.6 broadcast_in_dim.31.rate_ref
  243.9 0.6 broadcast_in_dim.28.length_ref
  244.5 0.6 broadcast_in_dim.29.rate_ref
  245.1 0.6 fusion.3
  245.7 0.6 fusion.2
  246.3 7.1 %pick_head.7 = bf16[1,2,96,512]{3,2,1,0:T(8,128)(2,1)} custom-call(s32[1]{0:T(128)} %bitcast.z_ref, bf16[2,96,512]{2,1,0:T(8,128)(2,1)} %get-tuple-element.33.rest_0_.rest_5_, bf16[2,96,512]{2,1,0:T(8,128)(2,1)} %copy-done.6, bf16[2,96,512]{2,1,0:T(8,128)(2,1)} %copy-done.8, bf16[2,96,512]{2,1,0:T(8,128)(2,1)} %copy-done.4), custom_call_target="tpu_custom_call" | custom-call | tf_op jit(solution)/shard_map/pick_head/pallas_call | solution.py:263
  253.4 7.1 %pick_head.6 = bf16[1,2,96,512]{3,2,1,0:T(8,128)(2,1)} custom-call(s32[1]{0:T(128)} %bitcast.z_ref, bf16[2,96,512]{2,1,0:T(8,128)(2,1)} %get-tuple-element.29.rest_0_.rest_5_, bf16[2,96,512]{2,1,0:T(8,128)(2,1)} %copy-done.5, bf16[2,96,512]{2,1,0:T(8,128)(2,1)} %copy-done.7, bf16[2,96,512]{2,1,0:T(8,128)(2,1)} %copy-done.9), custom_call_target="tpu_custom_call" | custom-call | tf_op jit(solution)/shard_map/pick_head/pallas_call | solution.py:263
  260.5 0.0 collective-permute-done.12.rest_1_.rest_6_
  260.5 1.9 collective-permute-start.11
  262.5 0.0 collective-permute-done.13.rest_2_.rest_7_
  262.5 16.6 %collective-permute-start.7 = (bf16[1,2,96,512]{3,2,1,0:T(8,128)(2,1)}, bf16[1,2,96,512]{3,2,1,0:T(8,128)(2,1)S(1)}, u32[]{:S(2)}, u32[]{:S(2)}) collective-permute-start(bf16[1,2,96,512]{3,2,1,0:T(8,128)(2,1)} %pick_head.6), channel_id=1, source_target_pairs={{1,0},{2,1},{3,2},{5,4},{6,5},{7,6},{9,8},{10,9},{11,10},{13,12},{... | collective-permute-start | bytes 589832 | tf_op jit(solution)/shard_map/ppermute | solution.py:402
  279.1 0.0 collective-permute-done.14.rest_3_.rest_8_
  279.1 0.8 copy-done.15
  279.9 19.0 %pick_head.8 = bf16[1,2,96,1536]{3,2,1,0:T(8,128)(2,1)} custom-call(s32[1]{0:T(128)} %bitcast.z_ref, bf16[2,96,1536]{2,1,0:T(8,128)(2,1)} %get-tuple-element.37.rest_0_.rest_5_, bf16[2,96,1536]{2,1,0:T(8,128)(2,1)} %copy-done.13, bf16[2,96,1536]{2,1,0:T(8,128)(2,1)} %copy-done.14, bf16[2,96,1536]{2,1,0:T(8,128)(2,1)} %copy-done.15), custom_call_target="tpu_custom_call" | custom-call | tf_op jit(solution)/shard_map/pick_head/pallas_call | solution.py:263
  298.9 1.9 collective-permute-start.15
  300.8 0.0 collective-permute-done.3.rest_4_
  300.8 0.0 collective-permute-done.19.rest_9_
  300.8 0.8 copy-done.3
  301.7 0.8 copy-done.20
  302.5 31.4 %azimuth_bins.4.rest_10_ = bf16[2,1,512,4096]{3,2,1,0:T(8,128)(2,1)} custom-call(s32[1]{0:T(128)} %bitcast.z_ref, s32[1,1536]{1,0:T(1,128)} %broadcast_in_dim.30.length_ref, f32[1,1536]{1,0:T(1,128)} %broadcast_in_dim.31.rate_ref, bf16[1280,1280]{1,0:T(8,128)(2,1)} %constant.24.clone.forward_ref, bf16[1024,1280]{1,0:T(8,128)(2,1)} %constant.25.clone.inverse_ref, ...), custom_call_target="tpu_custom_call" | custom-call | flops 9059696640 | bytes 7077888 | tf_op jit(solution)/shard_map/azimuth_bins/pallas_call | solution.py:362
  334.0 0.8 copy-done.21
  334.8 31.5 %azimuth_bins.5.rest_10_ = bf16[2,1,512,4096]{3,2,1,0:T(8,128)(2,1)} custom-call(s32[1]{0:T(128)} %bitcast.z_ref, s32[1,1536]{1,0:T(1,128)} %broadcast_in_dim.28.length_ref, f32[1,1536]{1,0:T(1,128)} %broadcast_in_dim.29.rate_ref, bf16[1280,1280]{1,0:T(8,128)(2,1)} %constant.24.clone.forward_ref, ...), custom_call_target="tpu_custom_call", output_to_operand_aliasing={{}: (15, {})} | custom-call | flops 9059696640 | bytes 7077888 | tf_op jit(solution)/shard_map/azimuth_bins/pallas_call | solution.py:362
  366.3 0.7 copy-done.17
  367.0 13.7 %azimuth_bins.6.rest_10_ = bf16[2,1,512,4096]{3,2,1,0:T(8,128)(2,1)} custom-call(s32[1]{0:T(128)} %bitcast.z_ref, s32[1,512]{1,0:T(1,128)} %bitcast.9, f32[1,512]{1,0:T(1,128)} %bitcast.10, bf16[1280,1280]{1,0:T(8,128)(2,1)} %constant.24.clone.forward_ref, bf16[1024,1280]{1,0:T(8,128)(2,1)} %constant.25.clone.inverse_ref, ...), custom_call_target="tpu_custom_call", output_to_operand_aliasing={{}: (15, {})} | custom-call | flops 3019898880 | bytes 2359296 | tf_op jit(solution)/shard_map/azimuth_bins/pallas_call | solution.py:362
  380.7 0.0 collective-permute-done.7.rest_9_
  380.7 0.7 copy-done.16
  381.4 13.5 %azimuth_bins.7 = bf16[2,1,512,4096]{3,2,1,0:T(8,128)(2,1)} custom-call(s32[1]{0:T(128)} %bitcast.z_ref, s32[1,512]{1,0:T(1,128)} %bitcast.7, f32[1,512]{1,0:T(1,128)} %bitcast.8, bf16[1280,1280]{1,0:T(8,128)(2,1)} %constant.24.clone.forward_ref, bf16[1024,1280]{1,0:T(8,128)(2,1)} %constant.25.clone.inverse_ref, ...), custom_call_target="tpu_custom_call", output_to_operand_aliasing={{}: (15, {})} | custom-call | flops 3019898880 | bytes 2359296 | tf_op jit(solution)/shard_map/azimuth_bins/pallas_call | solution.py:362
  (41 shorter events, 0.1 us)
Async XLA Ops:
  31.2 64.7 %copy-start.22 = (bf16[2,32,4096]{2,1,0:T(8,128)(2,1)S(1)}, bf16[2,32,4096]{2,1,0:T(8,128)(2,1)}, u32[]{:S(2)}) copy-start(bf16[2,32,4096]{2,1,0:T(8,128)(2,1)} %get-tuple-element.28) | copy-start | bytes 1572868
  31.2 164.6 %copy-start.18 = (s32[4096]{0:T(1024)S(1)}, s32[4096]{0:T(1024)}, u32[]{:S(2)}) copy-start(s32[4096]{0:T(1024)} %param.17) | copy-start | bytes 49156
  31.2 211.4 %copy-start.19 = (f32[4096]{0:T(1024)S(1)}, f32[4096]{0:T(1024)}, u32[]{:S(2)}) copy-start(f32[4096]{0:T(1024)} %param.18) | copy-start | bytes 49156
  31.3 64.7 %collective-permute-start = (bf16[2,32,4096]{2,1,0:T(8,128)(2,1)}, bf16[2,32,4096]{2,1,0:T(8,128)(2,1)S(1)}, u32[]{:S(2)}, u32[]{:S(2)}) collective-permute-start(bf16[2,32,4096]{2,1,0:T(8,128)(2,1)} %get-tuple-element.26), channel_id=1, source_target_pairs={{0,4},{4,0},{8,12},{12,8},{1,5},{5,1},{9,13},{13,9},{2,6},{6,2},{1... | collective-permute-start | bytes 1572872 | tf_op jit(solution)/shard_map/ppermute | solution.py:397
  83.1 7.6 %collective-permute-start.10 = (bf16[2,96,512]{2,1,0:T(8,128)(2,1)}, bf16[2,96,512]{2,1,0:T(8,128)(2,1)S(1)}, u32[]{:S(2)}, u32[]{:S(2)}) collective-permute-start(bf16[2,96,512]{2,1,0:T(8,128)(2,1)} %get-tuple-element.36), channel_id=1, source_target_pairs={{0,12},{4,8},{8,4},{12,0},{1,13},{5,9},{9,5},{13,1},{2,14},{6,10},... | collective-permute-start | bytes 589832 | tf_op jit(solution)/shard_map/ppermute | solution.py:397
  85.4 106.1 %collective-permute-start.16 = (bf16[2,96,1536]{2,1,0:T(8,128)(2,1)}, bf16[2,96,1536]{2,1,0:T(8,128)(2,1)S(1)}, u32[]{:S(2)}, u32[]{:S(2)}) collective-permute-start(bf16[2,96,1536]{2,1,0:T(8,128)(2,1)} %get-tuple-element.42), channel_id=1, source_target_pairs={{0,4},{4,0},{8,12},{12,8},{1,5},{5,1},{9,13},{13,9},{2,6},{6,2},{1... | collective-permute-start | bytes 1769480 | tf_op jit(solution)/shard_map/ppermute | solution.py:397
  85.8 105.7 %collective-permute-start.17 = (bf16[2,96,1536]{2,1,0:T(8,128)(2,1)}, bf16[2,96,1536]{2,1,0:T(8,128)(2,1)S(1)}, u32[]{:S(2)}, u32[]{:S(2)}) collective-permute-start(bf16[2,96,1536]{2,1,0:T(8,128)(2,1)} %get-tuple-element.43), channel_id=1, source_target_pairs={{0,8},{4,12},{8,0},{12,4},{1,9},{5,13},{9,1},{13,5},{2,10},{6,14},... | collective-permute-start | bytes 1769480 | tf_op jit(solution)/shard_map/ppermute | solution.py:397
  86.8 105.8 %collective-permute-start.18 = (bf16[2,96,1536]{2,1,0:T(8,128)(2,1)}, bf16[2,96,1536]{2,1,0:T(8,128)(2,1)S(1)}, u32[]{:S(2)}, u32[]{:S(2)}) collective-permute-start(bf16[2,96,1536]{2,1,0:T(8,128)(2,1)} %get-tuple-element.44), channel_id=1, source_target_pairs={{0,12},{4,8},{8,4},{12,0},{1,13},{5,9},{9,5},{13,1},{2,14},{6,10},... | collective-permute-start | bytes 1769480 | tf_op jit(solution)/shard_map/ppermute | solution.py:397
  90.8 155.5 %copy-start.4 = (bf16[2,96,512]{2,1,0:T(8,128)(2,1)}, bf16[2,96,512]{2,1,0:T(8,128)(2,1)S(1)}, u32[]{:S(2)}) copy-start(bf16[2,96,512]{2,1,0:T(8,128)(2,1)S(1)} %collective-permute-done.10.rest_3_.rest_8_) | copy-start | bytes 589828
  90.8 87.9 %collective-permute-start.1 = (bf16[2,32,4096]{2,1,0:T(8,128)(2,1)}, bf16[2,32,4096]{2,1,0:T(8,128)(2,1)S(1)}, u32[]{:S(2)}, u32[]{:S(2)}) collective-permute-start(bf16[2,32,4096]{2,1,0:T(8,128)(2,1)} %get-tuple-element.27), channel_id=1, source_target_pairs={{0,8},{4,12},{8,0},{12,4},{1,9},{5,13},{9,1},{13,5},{2,10},{6,14},... | collective-permute-start | bytes 1572872 | tf_op jit(solution)/shard_map/ppermute | solution.py:397
  95.9 99.9 %copy-start = (bf16[2,32,4096]{2,1,0:T(8,128)(2,1)}, bf16[2,32,4096]{2,1,0:T(8,128)(2,1)S(1)}, u32[]{:S(2)}) copy-start(bf16[2,32,4096]{2,1,0:T(8,128)(2,1)S(1)} %collective-permute-done.rest_1_) | copy-start | bytes 1572868
  95.9 82.7 %collective-permute-start.2 = (bf16[2,32,4096]{2,1,0:T(8,128)(2,1)S(1)}, bf16[2,32,4096]{2,1,0:T(8,128)(2,1)S(1)}, u32[]{:S(2)}, u32[]{:S(2)}) collective-permute-start(bf16[2,32,4096]{2,1,0:T(8,128)(2,1)S(1)} %copy-done.22), channel_id=1, source_target_pairs={{0,12},{4,8},{8,4},{12,0},{1,13},{5,9},{9,5},{13,1},{2,14},{6,10},... | collective-permute-start | bytes 1572872 | tf_op jit(solution)/shard_map/ppermute | solution.py:397
  178.6 17.2 %copy-start.1 = (bf16[2,32,4096]{2,1,0:T(8,128)(2,1)}, bf16[2,32,4096]{2,1,0:T(8,128)(2,1)S(1)}, u32[]{:S(2)}) copy-start(bf16[2,32,4096]{2,1,0:T(8,128)(2,1)S(1)} %collective-permute-done.1.rest_2_) | copy-start | bytes 1572868
  178.6 53.3 %collective-permute-start.8 = (bf16[2,96,512]{2,1,0:T(8,128)(2,1)}, bf16[2,96,512]{2,1,0:T(8,128)(2,1)S(1)}, u32[]{:S(2)}, u32[]{:S(2)}) collective-permute-start(bf16[2,96,512]{2,1,0:T(8,128)(2,1)} %get-tuple-element.34), channel_id=1, source_target_pairs={{0,4},{4,0},{8,12},{12,8},{1,5},{5,1},{9,13},{13,9},{2,6},{6,2},{1... | collective-permute-start | bytes 589832 | tf_op jit(solution)/shard_map/ppermute | solution.py:397
  178.6 17.2 %copy-start.2 = (bf16[2,32,4096]{2,1,0:T(8,128)(2,1)}, bf16[2,32,4096]{2,1,0:T(8,128)(2,1)S(1)}, u32[]{:S(2)}) copy-start(bf16[2,32,4096]{2,1,0:T(8,128)(2,1)S(1)} %collective-permute-done.2.rest_3_) | copy-start | bytes 1572868
  178.6 53.4 %collective-permute-start.9 = (bf16[2,96,512]{2,1,0:T(8,128)(2,1)}, bf16[2,96,512]{2,1,0:T(8,128)(2,1)S(1)}, u32[]{:S(2)}, u32[]{:S(2)}) collective-permute-start(bf16[2,96,512]{2,1,0:T(8,128)(2,1)} %get-tuple-element.35), channel_id=1, source_target_pairs={{0,8},{4,12},{8,0},{12,4},{1,9},{5,13},{9,1},{13,5},{2,10},{6,14},... | collective-permute-start | bytes 589832 | tf_op jit(solution)/shard_map/ppermute | solution.py:397
  191.5 21.4 %copy-start.10 = (bf16[2,96,1536]{2,1,0:T(8,128)(2,1)}, bf16[2,96,1536]{2,1,0:T(8,128)(2,1)S(1)}, u32[]{:S(2)}) copy-start(bf16[2,96,1536]{2,1,0:T(8,128)(2,1)S(1)} %collective-permute-done.16.rest_1_.rest_6_) | copy-start | bytes 1769476
  191.5 41.6 %collective-permute-start.4 = (bf16[2,96,512]{2,1,0:T(8,128)(2,1)}, bf16[2,96,512]{2,1,0:T(8,128)(2,1)S(1)}, u32[]{:S(2)}, u32[]{:S(2)}) collective-permute-start(bf16[2,96,512]{2,1,0:T(8,128)(2,1)} %get-tuple-element.30), channel_id=1, source_target_pairs={{0,4},{4,0},{8,12},{12,8},{1,5},{5,1},{9,13},{13,9},{2,6},{6,2},{1... | collective-permute-start | bytes 589832 | tf_op jit(solution)/shard_map/ppermute | solution.py:397
  191.5 21.4 %copy-start.11 = (bf16[2,96,1536]{2,1,0:T(8,128)(2,1)}, bf16[2,96,1536]{2,1,0:T(8,128)(2,1)S(1)}, u32[]{:S(2)}) copy-start(bf16[2,96,1536]{2,1,0:T(8,128)(2,1)S(1)} %collective-permute-done.17.rest_2_.rest_7_) | copy-start | bytes 1769476
  191.5 44.0 %collective-permute-start.5 = (bf16[2,96,512]{2,1,0:T(8,128)(2,1)}, bf16[2,96,512]{2,1,0:T(8,128)(2,1)S(1)}, u32[]{:S(2)}, u32[]{:S(2)}) collective-permute-start(bf16[2,96,512]{2,1,0:T(8,128)(2,1)} %get-tuple-element.31), channel_id=1, source_target_pairs={{0,8},{4,12},{8,0},{12,4},{1,9},{5,13},{9,1},{13,5},{2,10},{6,14},... | collective-permute-start | bytes 589832 | tf_op jit(solution)/shard_map/ppermute | solution.py:397
  192.5 0.8 copy-start.12
  193.3 47.4 %collective-permute-start.6 = (bf16[2,96,512]{2,1,0:T(8,128)(2,1)}, bf16[2,96,512]{2,1,0:T(8,128)(2,1)S(1)}, u32[]{:S(2)}, u32[]{:S(2)}) collective-permute-start(bf16[2,96,512]{2,1,0:T(8,128)(2,1)} %get-tuple-element.32), channel_id=1, source_target_pairs={{0,12},{4,8},{8,4},{12,0},{1,13},{5,9},{9,5},{13,1},{2,14},{6,10},... | collective-permute-start | bytes 589832 | tf_op jit(solution)/shard_map/ppermute | solution.py:397
  231.9 14.4 %copy-start.6 = (bf16[2,96,512]{2,1,0:T(8,128)(2,1)}, bf16[2,96,512]{2,1,0:T(8,128)(2,1)S(1)}, u32[]{:S(2)}) copy-start(bf16[2,96,512]{2,1,0:T(8,128)(2,1)S(1)} %collective-permute-done.8.rest_1_.rest_6_) | copy-start | bytes 589828
  231.9 28.6 %collective-permute-start.12 = (bf16[2,96,1536]{2,1,0:T(8,128)(2,1)}, bf16[2,96,1536]{2,1,0:T(8,128)(2,1)S(1)}, u32[]{:S(2)}, u32[]{:S(2)}) collective-permute-start(bf16[2,96,1536]{2,1,0:T(8,128)(2,1)} %get-tuple-element.38), channel_id=1, source_target_pairs={{0,4},{4,0},{8,12},{12,8},{1,5},{5,1},{9,13},{13,9},{2,6},{6,2},{1... | collective-permute-start | bytes 1769480 | tf_op jit(solution)/shard_map/ppermute | solution.py:397
  232.0 14.3 %copy-start.8 = (bf16[2,96,512]{2,1,0:T(8,128)(2,1)}, bf16[2,96,512]{2,1,0:T(8,128)(2,1)S(1)}, u32[]{:S(2)}) copy-start(bf16[2,96,512]{2,1,0:T(8,128)(2,1)S(1)} %collective-permute-done.9.rest_2_.rest_7_) | copy-start | bytes 589828
  232.0 30.4 %collective-permute-start.13 = (bf16[2,96,1536]{2,1,0:T(8,128)(2,1)}, bf16[2,96,1536]{2,1,0:T(8,128)(2,1)S(1)}, u32[]{:S(2)}, u32[]{:S(2)}) collective-permute-start(bf16[2,96,1536]{2,1,0:T(8,128)(2,1)} %get-tuple-element.39), channel_id=1, source_target_pairs={{0,8},{4,12},{8,0},{12,4},{1,9},{5,13},{9,1},{13,5},{2,10},{6,14},... | collective-permute-start | bytes 1769480 | tf_op jit(solution)/shard_map/ppermute | solution.py:397
  233.0 20.4 %copy-start.5 = (bf16[2,96,512]{2,1,0:T(8,128)(2,1)}, bf16[2,96,512]{2,1,0:T(8,128)(2,1)S(1)}, u32[]{:S(2)}) copy-start(bf16[2,96,512]{2,1,0:T(8,128)(2,1)S(1)} %collective-permute-done.4.rest_1_.rest_6_) | copy-start | bytes 589828
  233.0 46.0 %collective-permute-start.14 = (bf16[2,96,1536]{2,1,0:T(8,128)(2,1)}, bf16[2,96,1536]{2,1,0:T(8,128)(2,1)S(1)}, u32[]{:S(2)}, u32[]{:S(2)}) collective-permute-start(bf16[2,96,1536]{2,1,0:T(8,128)(2,1)} %get-tuple-element.40), channel_id=1, source_target_pairs={{0,12},{4,8},{8,4},{12,0},{1,13},{5,9},{9,5},{13,1},{2,14},{6,10},... | collective-permute-start | bytes 1769480 | tf_op jit(solution)/shard_map/ppermute | solution.py:397
  235.5 17.9 %copy-start.7 = (bf16[2,96,512]{2,1,0:T(8,128)(2,1)}, bf16[2,96,512]{2,1,0:T(8,128)(2,1)S(1)}, u32[]{:S(2)}) copy-start(bf16[2,96,512]{2,1,0:T(8,128)(2,1)S(1)} %collective-permute-done.5.rest_2_.rest_7_) | copy-start | bytes 589828
  235.5 65.3 %collective-permute-start.3 = (bf16[1,2,32,4096]{3,2,1,0:T(8,128)(2,1)}, bf16[1,2,32,4096]{3,2,1,0:T(8,128)(2,1)S(1)}, u32[]{:S(2)}, u32[]{:S(2)}) collective-permute-start(bf16[1,2,32,4096]{3,2,1,0:T(8,128)(2,1)} %pick_head.5), channel_id=1, source_target_pairs={{1,0},{2,1},{3,2},{5,4},{6,5},{7,6},{9,8},{10,9},{11,10},{13,12},{... | collective-permute-start | bytes 1572872 | tf_op jit(solution)/shard_map/ppermute | solution.py:402
  240.8 12.7 %copy-start.9 = (bf16[2,96,512]{2,1,0:T(8,128)(2,1)}, bf16[2,96,512]{2,1,0:T(8,128)(2,1)S(1)}, u32[]{:S(2)}) copy-start(bf16[2,96,512]{2,1,0:T(8,128)(2,1)S(1)} %collective-permute-done.6.rest_3_.rest_8_) | copy-start | bytes 589828
  240.8 60.1 %collective-permute-start.19 = (bf16[1,2,96,1536]{3,2,1,0:T(8,128)(2,1)}, bf16[1,2,96,1536]{3,2,1,0:T(8,128)(2,1)S(1)}, u32[]{:S(2)}, u32[]{:S(2)}) collective-permute-start(bf16[1,2,96,1536]{3,2,1,0:T(8,128)(2,1)} %pick_head.9), channel_id=1, source_target_pairs={{1,0},{2,1},{3,2},{5,4},{6,5},{7,6},{9,8},{10,9},{11,10},{13,12},{... | collective-permute-start | bytes 1769480 | tf_op jit(solution)/shard_map/ppermute | solution.py:402
  260.5 18.6 %copy-start.13 = (bf16[2,96,1536]{2,1,0:T(8,128)(2,1)}, bf16[2,96,1536]{2,1,0:T(8,128)(2,1)S(1)}, u32[]{:S(2)}) copy-start(bf16[2,96,1536]{2,1,0:T(8,128)(2,1)S(1)} %collective-permute-done.12.rest_1_.rest_6_) | copy-start | bytes 1769476
  260.5 105.8 %collective-permute-start.11 = (bf16[1,2,96,512]{3,2,1,0:T(8,128)(2,1)}, bf16[1,2,96,512]{3,2,1,0:T(8,128)(2,1)S(1)}, u32[]{:S(2)}, u32[]{:S(2)}) collective-permute-start(bf16[1,2,96,512]{3,2,1,0:T(8,128)(2,1)} %pick_head.7), channel_id=1, source_target_pairs={{1,0},{2,1},{3,2},{5,4},{6,5},{7,6},{9,8},{10,9},{11,10},{13,12},{... | collective-permute-start | bytes 589832 | tf_op jit(solution)/shard_map/ppermute | solution.py:402
  262.5 16.7 %copy-start.14 = (bf16[2,96,1536]{2,1,0:T(8,128)(2,1)}, bf16[2,96,1536]{2,1,0:T(8,128)(2,1)S(1)}, u32[]{:S(2)}) copy-start(bf16[2,96,1536]{2,1,0:T(8,128)(2,1)S(1)} %collective-permute-done.13.rest_2_.rest_7_) | copy-start | bytes 1769476
  262.5 118.2 %collective-permute-start.7 = (bf16[1,2,96,512]{3,2,1,0:T(8,128)(2,1)}, bf16[1,2,96,512]{3,2,1,0:T(8,128)(2,1)S(1)}, u32[]{:S(2)}, u32[]{:S(2)}) collective-permute-start(bf16[1,2,96,512]{3,2,1,0:T(8,128)(2,1)} %pick_head.6), channel_id=1, source_target_pairs={{1,0},{2,1},{3,2},{5,4},{6,5},{7,6},{9,8},{10,9},{11,10},{13,12},{... | collective-permute-start | bytes 589832 | tf_op jit(solution)/shard_map/ppermute | solution.py:402
  279.1 0.8 copy-start.15
  298.9 35.1 %collective-permute-start.15 = (bf16[1,2,96,1536]{3,2,1,0:T(8,128)(2,1)}, bf16[1,2,96,1536]{3,2,1,0:T(8,128)(2,1)S(1)}, u32[]{:S(2)}, u32[]{:S(2)}) collective-permute-start(bf16[1,2,96,1536]{3,2,1,0:T(8,128)(2,1)} %pick_head.8), channel_id=1, source_target_pairs={{1,0},{2,1},{3,2},{5,4},{6,5},{7,6},{9,8},{10,9},{11,10},{13,12},{... | collective-permute-start | bytes 1769480 | tf_op jit(solution)/shard_map/ppermute | solution.py:402
  300.8 0.9 copy-start.3
  301.7 0.8 copy-start.20
  334.0 0.8 copy-start.21
  366.3 0.7 copy-start.17
  380.7 0.7 copy-start.16
